TPU v7x, 256 devices: a whole 4x4x8 slice. The times are simulated.
256 devices in a mesh: row: 16 (over y, z_hi, core), col: 16 (over x, z_lo).
Axes of the slice: x: 4, y: 4, z: 8 (z_hi: 2, z_lo: 4; z = z_hi * 4 + z_lo), core: 2. Of those that a mesh axis runs over, the one named last changes fastest.
Arguments:
- features: bfloat16 [131072, 128], P(('col', 'row')), may hold values from -6 to 6
- weight: bfloat16 [128, 256], replicated, may hold values from -0.5 to 0.5
- cotangent: bfloat16 [131072, 256], P(('row', 'col')), may hold values from -6 to 6
- adj_blocks: bfloat16 [16, 16, 256, 128, 128], P('row', 'col'), may hold values from -0.0625 to 0.0625
- block_rows: int32 [16, 16, 256], P('row', 'col'), may hold values from 0 to 63, as said below
- block_cols: int32 [16, 16, 256], P('row', 'col'), may hold values from 0 to 63, as said below
- live_mask: int32 [16, 16, 256], P('row', 'col'), may hold values from 0 to 1, as said below
Outputs:
- activated: bfloat16 [131072, 256], P(('row', 'col'))
- grad_input: bfloat16 [131072, 128], P(('col', 'row'))
- grad_weight: float32 [128, 256], replicated
Inputs may be any that keep to these rules, and one draw needn't show every extreme that they name: `block_rows`: within one tile the 256 slots name distinct blocks. `block_cols`: together with block_rows, distinct blocks within one tile. `live_mask`: in each tile the live slots come first; every slot is live on each tile whose node row range and node column range meet.
All inputs are finite; a program needn't handle non-finite values.
Results may differ from a plain program's by a relative error of at most 0.0049.
Values may be sent and summed in bfloat16 or wider, within the bound.
A program may use at most 128 MiB of HBM per device.

v0:
```python
import math

import jax
import jax.numpy as jnp
from jax import lax
from jax.sharding import PartitionSpec as P


def spread(values, pick_ids, put_ids, live_slots, source, put_count, transpose, group_count):
    slots = values.shape[0]
    group_size = min(64, slots)
    block_size = values.shape[1]
    columns = source.shape[1]
    blocked = source.reshape(-1, block_size, columns)
    einsum_form = "kji,kjw->kiw" if transpose else "kij,kjw->kiw"

    def one_turn(turn, total):
        start = turn * group_size
        tile_vals = lax.dynamic_slice_in_dim(values, start, group_size, 0)
        picks = lax.dynamic_slice_in_dim(pick_ids, start, group_size, 0)
        places = lax.dynamic_slice_in_dim(put_ids, start, group_size, 0)
        alive = lax.dynamic_slice_in_dim(live_slots, start, group_size, 0)
        gathered = jnp.take(blocked, picks, axis=0)
        product = jnp.einsum(einsum_form, tile_vals, gathered, preferred_element_type=jnp.float32)
        product = product * alive.astype(jnp.float32)[:, None, None]
        return total.at[places].add(product)

    total = lax.fori_loop(
        0, group_count, one_turn, jnp.zeros((put_count, block_size, columns), jnp.float32)
    )
    return total.reshape(put_count * block_size, columns)


def on_device(features, weight, cotangent, adj_blocks, block_rows, block_cols, live_mask):
    tile_vals = adj_blocks[0, 0]
    row_ids = block_rows[0, 0]
    col_ids = block_cols[0, 0]
    live_slots = live_mask[0, 0]
    block_size = tile_vals.shape[1]
    slots = tile_vals.shape[0]
    group_size = min(64, slots)
    tile_rows = cotangent.shape[0] * lax.axis_size("col") // block_size
    tile_cols = features.shape[0] * lax.axis_size("row") // block_size
    nodes = features.shape[0] * lax.axis_size("row") * lax.axis_size("col")
    group_count = slots // group_size
    gathered = lax.all_gather(features, "row", axis=0, tiled=True)
    partial_value = spread(
        tile_vals, col_ids, row_ids, live_slots, gathered, tile_rows, False, group_count
    )
    aggregated = lax.psum_scatter(partial_value, "col", scatter_dimension=0, tiled=True)
    weight_wide = weight.astype(jnp.float32)
    pre = jnp.dot(aggregated, weight_wide, precision=lax.Precision.HIGHEST)
    activated = jax.nn.silu(pre).astype(jnp.bfloat16)
    sigmoid = jax.nn.sigmoid(pre)
    grad_pre = (cotangent.astype(jnp.float32) * sigmoid * (1.0 + pre * (1.0 - sigmoid))).astype(
        jnp.bfloat16
    )
    spread_rows = lax.all_gather(grad_pre, "col", axis=0, tiled=True)
    backward = spread(
        tile_vals, row_ids, col_ids, live_slots, spread_rows, tile_cols, True, group_count
    )
    grad_nodes = lax.psum_scatter(backward, "row", scatter_dimension=0, tiled=True)
    grad_input = jnp.dot(grad_nodes, weight_wide.T, precision=lax.Precision.HIGHEST).astype(
        jnp.bfloat16
    )
    local_term = jnp.dot(
        features.astype(jnp.float32).T, grad_nodes, precision=lax.Precision.HIGHEST
    )
    grad_weight = lax.psum(local_term, ("row", "col")) * (1.0 / math.sqrt(nodes))
    return (activated, grad_input, grad_weight)


def solution(mesh):
    in_specs = (
        P(("col", "row"), None),
        P(),
        P(("row", "col"), None),
        P("row", "col", None, None, None),
        P("row", "col", None),
        P("row", "col", None),
        P("row", "col", None),
    )
    out_specs = (P(("row", "col"), None), P(("col", "row"), None), P())
    return jax.shard_map(
        on_device, mesh=mesh, in_specs=in_specs, out_specs=out_specs, check_vma=False
    )
```

profile of v0, /device:TPU:1, one launch (start us, length us, event | category | flops | bytes accessed | tf_op | source)
XLA Modules:
  0.0 886.8 jit_solution(9825797443615405362)
XLA Ops:
  8.0 69.9 %all-gather.3.cloned.1.call-done = bf16[8192,128]{1,0:T(8,128)(2,1)} async-done(((bf16[512,128]{1,0:T(8,128)(2,1)}), bf16[8192,128]{1,0:T(8,128)(2,1)}) %all-gather.3.cloned.1.call-update) | async-done | bytes 2097168 | tf_op jit(solution)/shard_map/all_gather | solution.py:46
  80.4 82.2 %while.26 = (s32[]{:T(128)}, f32[64,128,128]{2,1,0:T(8,128)}, s32[256]{0:T(256)S(1)}, bf16[256,128,128]{2,1,0:T(8,128)(2,1)}, s32[256]{0:T(256)S(1)}, /*index=5*...) while((s32[]{:T(128)}, f32[64,128,128]{2,1,0:T(8,128)}, ...), condition=%wide.region_2.3_spmd, body=%wide.region_0.2_spmd.sunk | while | flops 271582848 | bytes 25172776 | solution.py:28
  87.5 13.5 %scatter_fusion = f32[64,128,128]{2,1,0:T(8,128)} fusion(f32[64,128,128]{2,1,0:T(8,128)} %get-tuple-element.415, s32[64]{0:T(128)S(1)} %get-tuple-element.388, f32[64,128,128]{2,1,0:T(8,128)} %convolution_multiply_fusion.2), kind=kCustom, calls=%fused_computation.2.clone.1 | custom fusion | flops 1048576 | bytes 12583168 | tf_op jit(solution)/shard_map/while/body/eval_jaxpr/scatter-add | solution.py:26
  108.0 13.5 %scatter_fusion = f32[64,128,128]{2,1,0:T(8,128)} fusion(f32[64,128,128]{2,1,0:T(8,128)} %get-tuple-element.415, s32[64]{0:T(128)S(1)} %get-tuple-element.388, f32[64,128,128]{2,1,0:T(8,128)} %convolution_multiply_fusion.2), kind=kCustom, calls=%fused_computation.2.clone.1 | custom fusion | flops 1048576 | bytes 12583168 | tf_op jit(solution)/shard_map/while/body/eval_jaxpr/scatter-add | solution.py:26
  128.5 13.5 %scatter_fusion = f32[64,128,128]{2,1,0:T(8,128)} fusion(f32[64,128,128]{2,1,0:T(8,128)} %get-tuple-element.415, s32[64]{0:T(128)S(1)} %get-tuple-element.388, f32[64,128,128]{2,1,0:T(8,128)} %convolution_multiply_fusion.2), kind=kCustom, calls=%fused_computation.2.clone.1 | custom fusion | flops 1048576 | bytes 12583168 | tf_op jit(solution)/shard_map/while/body/eval_jaxpr/scatter-add | solution.py:26
  149.1 13.6 %scatter_fusion = f32[64,128,128]{2,1,0:T(8,128)} fusion(f32[64,128,128]{2,1,0:T(8,128)} %get-tuple-element.415, s32[64]{0:T(128)S(1)} %get-tuple-element.388, f32[64,128,128]{2,1,0:T(8,128)} %convolution_multiply_fusion.2), kind=kCustom, calls=%fused_computation.2.clone.1 | custom fusion | flops 1048576 | bytes 12583168 | tf_op jit(solution)/shard_map/while/body/eval_jaxpr/scatter-add | solution.py:26
  162.7 95.2 %reduce-scatter.3.cloned.1.call-done = f32[512,128]{1,0:T(8,128)} async-done(((f32[8192,128]{1,0:T(8,128)}), f32[512,128]{1,0:T(8,128)}) %reduce-scatter.3.cloned.1.call-update) | async-done | bytes 262160 | tf_op jit(solution)/shard_map/reduce_scatter | solution.py:50
  260.3 12.0 %copy.10 = bf16[1,1,256,128,128]{3,4,2,1,0:T(8,128)(2,1)} copy(bf16[1,1,256,128,128]{4,3,2,1,0:T(8,128)(2,1)} %bitcast.22) | data formatting | bytes 16777216 | tf_op args[3]
  272.3 90.4 %all-gather.5.cloned.1.call-done = bf16[8192,256]{1,0:T(8,128)(2,1)} async-done(((bf16[512,256]{1,0:T(8,128)(2,1)}), bf16[8192,256]{1,0:T(8,128)(2,1)}) %all-gather.5.cloned.1.call-update) | async-done | bytes 4194320 | tf_op jit(solution)/shard_map/all_gather | solution.py:58
  367.0 128.1 %while.27 = (s32[]{:T(128)}, f32[64,128,256]{2,1,0:T(8,128)}, s32[256]{0:T(256)S(1)}, bf16[256,128,128]{1,2,0:T(8,128)(2,1)}, s32[256]{0:T(256)S(1)}, /*index=5*...) while((s32[]{:T(128)}, f32[64,128,256]{2,1,0:T(8,128)}, ...), condition=%wide.region_6.7_spmd, body=%wide.region_4.6_spmd.sunk | while | flops 543164032 | bytes 48241448 | solution.py:28
  367.1 4.9 gather_fusion.1
  372.0 7.4 broadcast_multiply_fusion.3
  379.4 19.6 %scatter_fusion.1 = f32[64,128,256]{2,1,0:T(8,128)} fusion(f32[64,128,256]{2,1,0:T(8,128)} %get-tuple-element.448, s32[64]{0:T(128)S(1)} %get-tuple-element.399, f32[64,128,256]{2,1,0:T(8,128)} %broadcast_multiply_fusion.3), kind=kCustom, calls=%fused_computation.3.clone.1 | custom fusion | flops 2097152 | bytes 25166080 | tf_op jit(solution)/shard_map/while/body/eval_jaxpr/scatter-add | solution.py:26
  399.1 4.9 gather_fusion.1
  404.1 7.4 broadcast_multiply_fusion.3
  411.4 19.4 %scatter_fusion.1 = f32[64,128,256]{2,1,0:T(8,128)} fusion(f32[64,128,256]{2,1,0:T(8,128)} %get-tuple-element.448, s32[64]{0:T(128)S(1)} %get-tuple-element.399, f32[64,128,256]{2,1,0:T(8,128)} %broadcast_multiply_fusion.3), kind=kCustom, calls=%fused_computation.3.clone.1 | custom fusion | flops 2097152 | bytes 25166080 | tf_op jit(solution)/shard_map/while/body/eval_jaxpr/scatter-add | solution.py:26
  431.0 4.9 gather_fusion.1
  436.0 7.4 broadcast_multiply_fusion.3
  443.4 19.7 %scatter_fusion.1 = f32[64,128,256]{2,1,0:T(8,128)} fusion(f32[64,128,256]{2,1,0:T(8,128)} %get-tuple-element.448, s32[64]{0:T(128)S(1)} %get-tuple-element.399, f32[64,128,256]{2,1,0:T(8,128)} %broadcast_multiply_fusion.3), kind=kCustom, calls=%fused_computation.3.clone.1 | custom fusion | flops 2097152 | bytes 25166080 | tf_op jit(solution)/shard_map/while/body/eval_jaxpr/scatter-add | solution.py:26
  463.2 4.9 gather_fusion.1
  468.1 7.4 broadcast_multiply_fusion.3
  475.5 19.6 %scatter_fusion.1 = f32[64,128,256]{2,1,0:T(8,128)} fusion(f32[64,128,256]{2,1,0:T(8,128)} %get-tuple-element.448, s32[64]{0:T(128)S(1)} %get-tuple-element.399, f32[64,128,256]{2,1,0:T(8,128)} %broadcast_multiply_fusion.3), kind=kCustom, calls=%fused_computation.3.clone.1 | custom fusion | flops 2097152 | bytes 25166080 | tf_op jit(solution)/shard_map/while/body/eval_jaxpr/scatter-add | solution.py:26
  495.1 139.7 %reduce-scatter.5.cloned.1.call-done = f32[512,256]{1,0:T(8,128)} async-done(((f32[8192,256]{1,0:T(8,128)}), f32[512,256]{1,0:T(8,128)}) %reduce-scatter.5.cloned.1.call-update) | async-done | bytes 524304 | tf_op jit(solution)/shard_map/reduce_scatter | solution.py:62
  639.3 239.3 %all-reduce.2.cloned.1.call-done = f32[128,256]{0,1:T(8,128)} async-done(((f32[128,256]{0,1:T(8,128)}), f32[128,256]{0,1:T(8,128)}) %all-reduce.2.cloned.1.call-update) | async-done | bytes 131088 | tf_op jit(solution)/shard_map/psum | solution.py:69
  (61 shorter events, 44.8 us)
Async XLA Ops:
  7.2 250.8 %copy-start = (bf16[128,256]{1,0:T(8,128)(2,1)S(1)}, bf16[128,256]{1,0:T(8,128)(2,1)}, u32[]{:S(2)}) copy-start(bf16[128,256]{1,0:T(8,128)(2,1)} %param.12) | copy-start | bytes 196612
  7.2 73.2 %copy-start.2 = (s32[1,1,256]{2,1,0:T(1,128)S(1)}, s32[1,1,256]{2,1,0:T(1,128)}, u32[]{:S(2)}) copy-start(s32[1,1,256]{2,1,0:T(1,128)} %param.17) | copy-start | bytes 3076
  7.2 73.2 %copy-start.4 = (s32[1,1,256]{2,1,0:T(1,128)S(1)}, s32[1,1,256]{2,1,0:T(1,128)}, u32[]{:S(2)}) copy-start(s32[1,1,256]{2,1,0:T(1,128)} %param.16) | copy-start | bytes 3076
  7.2 73.2 %copy-start.3 = (s32[1,1,256]{2,1,0:T(1,128)S(1)}, s32[1,1,256]{2,1,0:T(1,128)}, u32[]{:S(2)}) copy-start(s32[1,1,256]{2,1,0:T(1,128)} %param.15) | copy-start | bytes 3076
  7.2 70.7 %all-gather.3.cloned.1.call-start = ((), (), s32[]{:S(2)}) async-start(), calls=%async_computation.2 | async-start | bytes 2228224 | tf_op jit(solution)/shard_map/all_gather | solution.py:46
  7.9 250.0 %reduce-scatter.3.cloned.1.call-start = ((), (), s32[]{:S(2)}) async-start(), calls=%async_computation.3 | async-start | bytes 4456448 | tf_op jit(solution)/shard_map/reduce_scatter | solution.py:50
  162.6 95.3 %copy-start.5 = (bf16[512,256]{1,0:T(8,128)(2,1)S(1)}, bf16[512,256]{1,0:T(8,128)(2,1)}, u32[]{:S(2)}) copy-start(bf16[512,256]{1,0:T(8,128)(2,1)} %param.13) | copy-start | bytes 786436
  162.7 200.0 %all-gather.5.cloned.1.call-start = ((), (), s32[]{:S(2)}) async-start(), calls=%async_computation.4 | async-start | bytes 4456448 | tf_op jit(solution)/shard_map/all_gather | solution.py:58
  260.2 374.6 %reduce-scatter.5.cloned.1.call-start = ((), (), s32[]{:S(2)}) async-start(), calls=%async_computation.5 | async-start | bytes 8912896 | tf_op jit(solution)/shard_map/reduce_scatter | solution.py:62
  495.1 139.8 %copy-start.1 = (bf16[512,128]{1,0:T(8,128)(2,1)S(1)}, bf16[512,128]{1,0:T(8,128)(2,1)}, u32[]{:S(2)}) copy-start(bf16[512,128]{1,0:T(8,128)(2,1)} %param.11) | copy-start | bytes 393220
  495.1 383.4 %all-reduce.2.cloned.1.call-start = ((), (), s32[]{:S(2)}) async-start(), calls=%async_computation.6 | async-start | bytes 262144 | tf_op jit(solution)/shard_map/psum | solution.py:69
Sparse Core Ops, SparseCore 0:
  10.7 67.1 all-gather.2
  162.8 95.1 reduce-scatter.2
  260.4 102.2 all-gather.4
  495.2 139.5 reduce-scatter.4
  640.8 237.7 all-reduce.1
where the time goes:
time: 889 us; the launch traced here: 887 us
  waiting for transfers between devices  635 us (71%)
  other arithmetic  134 us (15%)
  matrix products  53.5 us (6%)
  local copies, waits for them, and re-layouts  49.4 us (6%)
  between operations  13.8 us (2%)
    psum x1, waiting for transfers between devices, on_device(): lax.psum(local_term, ('row', 'col')) * (1.0 / math.sqrt(nodes))  239 us
    reduce_scatter x1, waiting for transfers between devices, on_device(): lax.psum_scatter(backward, 'row', scatter_dimension=0, tiled=True)  140 us
    scatter-add x8, other arithmetic, one_turn(): return total.at[places].add(product)  132 us
    reduce_scatter x1, waiting for transfers between devices, on_device(): lax.psum_scatter(partial_value, 'col', scatter_dimension=0, tiled=True)  95.2 us
    all_gather x1, waiting for transfers between devices, on_device(): spread_rows = lax.all_gather(grad_pre, 'col', axis=0, tiled=True)  90.4 us
    all_gather x1, waiting for transfers between devices, on_device(): gathered = lax.all_gather(features, 'row', axis=0, tiled=True)  69.9 us
    dot_general x8, matrix products, one_turn(): jnp.einsum(einsum_form, tile_vals, gathered, preferred_element_type=jnp.f...  46.8 us
    gather x8, local copies, waits for them, and re-layouts, one_turn(): gathered = jnp.take(blocked, picks, axis=0)  29.9 us
  transfers between devices with their start and end apart: 5, of which 5 were waited for; matrix products, arithmetic and copies ran while one was open for 2% of the time, Pallas kernels for 0%

commit v1 on v0

v1 whole, which is shorter than its diff:
```python
import functools
import math

import jax
import jax.numpy as jnp
from jax import lax
from jax.experimental import pallas as pl
from jax.experimental.pallas import tpu as pltpu
from jax.sharding import PartitionSpec as P

MESH = pl.DeviceIdType.MESH
BF = jnp.bfloat16
F32 = jnp.float32
BLK = 128
SLOTS = 256
BLOCKS = 64
UNROLL = 32


def slot_tables(put, pick, live):
    shape = (SLOTS, SLOTS)
    put_lane = jnp.broadcast_to(jnp.where(live != 0, put, BLOCKS), shape)
    put_sub = put_lane.T
    pick_sub = jnp.broadcast_to(pick, shape).T
    sub = lax.broadcasted_iota(jnp.int32, shape, 0)
    lane = lax.broadcasted_iota(jnp.int32, shape, 1)

    def count(mask, axis):
        return jnp.sum(mask.astype(jnp.int32), axis=axis, keepdims=True)

    rank = count(put_lane * SLOTS + lane < put_sub * SLOTS + sub, 1)
    chosen = rank == lane
    continues = count((put_lane == put_sub) & (lane < sub), 1) > 0
    order = jnp.sum(jnp.where(chosen, sub, 0), axis=0, keepdims=True)
    source = jnp.sum(jnp.where(chosen, pick_sub, 0), axis=0, keepdims=True)
    follow = count(chosen & continues, 0)
    held = count(put_sub == lane, 0)
    upto = count(put_sub <= lane, 0)
    last = jnp.where(held > 0, upto - 1, SLOTS)
    return order, source, follow, last


def kernel(
    feat, weight, cot, adj, rows, cols, live,
    act_out, gi_out, gw_out,
    a_v, x_v, s_v, p_v, g_v, p2_v, w_v, cot_v, act_v, gp_v, hi_v, lo_v, gi_v,
    rl, rr, rxl, rxr, zs, rz, tz,
    sib, rl2, rr2, rxl2, rxr2, zs2, rz2,
    gwp, gx, g1, gz, gy, g3, gc, g4, gh, gwf,
    tab_v, tab, send_sem, recv_sem, local_sem,
):
    row = lax.axis_index("row")
    col = lax.axis_index("col")
    y, h, c = row // 4, (row // 2) % 2, row % 2
    x, z = col // 4, col % 4
    xr, xo, xl = (x + 1) % 4, (x + 2) % 4, (x + 3) % 4
    yr, yo, yl = (y + 1) % 4, (y + 2) % 4, (y + 3) % 4

    def col_dev(x_, z_):
        return (row, x_ * 4 + z_)

    def row_of(y_, h_, c_):
        return y_ * 4 + h_ * 2 + c_

    def row_dev(y_, h_, c_):
        return (row_of(y_, h_, c_), col)

    peers = [col_dev(xr, z), col_dev(xo, z), col_dev(xl, z)]
    peers += [col_dev(x, (z + d) % 4) for d in (1, 2, 3)]
    peers += [row_dev(yr, h, c), row_dev(yo, h, c), row_dev(yl, h, c)]
    peers += [row_dev(y, 1 - h, c), row_dev(y, h, 1 - c)]
    barrier = pltpu.get_barrier_semaphore()
    for peer in peers:
        pl.semaphore_signal(barrier, inc=1, device_id=peer, device_id_type=MESH)

    names = {}
    pending = []

    def number(name):
        return names.setdefault(name, len(names))

    def send(name, src, dst, device):
        k = number(name)
        copy = pltpu.make_async_remote_copy(
            src_ref=src, dst_ref=dst, send_sem=send_sem.at[k], recv_sem=recv_sem.at[k],
            device_id=device, device_id_type=MESH,
        )
        copy.start()
        pending.append(copy)

    def recv(name, dst, device):
        k = number(name)
        pltpu.make_async_remote_copy(
            src_ref=dst, dst_ref=dst, send_sem=send_sem.at[k], recv_sem=recv_sem.at[k],
            device_id=device, device_id_type=MESH,
        ).wait_recv()

    def flush():
        while pending:
            pending.pop(0).wait_send()

    load_a = pltpu.make_async_copy(adj, a_v, local_sem.at[0])
    load_a.start()
    load_w = pltpu.make_async_copy(weight, w_v, local_sem.at[1])
    load_w.start()
    load_c = pltpu.make_async_copy(cot, cot_v, local_sem.at[2])
    load_c.start()

    def part(ref, chunk, lo=0, hi=4):
        return ref.at[pl.ds(chunk * 4 + lo, hi - lo)]

    own = part(x_v, row)
    load_f = pltpu.make_async_copy(feat, own, local_sem.at[3])
    load_f.start()
    pl.semaphore_wait(barrier, len(peers))

    send("Az", feat, own, row_dev(y, 1 - h, c))
    send("Ar0", feat, own, row_dev(yr, h, c))
    send("Al0", feat, own, row_dev(yl, h, c))
    send("As", feat, own, row_dev(y, h, 1 - c))

    table = slot_tables(rows[...], cols[...], live[...])
    for k in range(4):
        tab_v[k : k + 1, :] = table[k]
    table = slot_tables(cols[...], rows[...], live[...])
    for k in range(4):
        tab_v[k + 4 : k + 5, :] = table[k]
    load_t = pltpu.make_async_copy(tab_v, tab, local_sem.at[4])
    load_t.start()
    s_v[SLOTS] = jnp.zeros((BLK, BLK), F32)

    sibling = row_dev(y, h, 1 - c)

    def share(name, chunk, lo=0, hi=4):
        send("S" + name, part(x_v, chunk, lo, hi), part(x_v, chunk, lo, hi), sibling)

    left, right = row_of(yl, h, c), row_of(yr, h, c)
    recv("Ar0", part(x_v, left), row_dev(yl, h, c))
    send("Arr", part(x_v, left, 0, 2), part(x_v, left, 0, 2), row_dev(yr, h, c))
    share("l0", left)
    recv("Al0", part(x_v, right), row_dev(yr, h, c))
    send("All", part(x_v, right, 2, 4), part(x_v, right, 2, 4), row_dev(yl, h, c))
    share("r0", right)
    across = row_of(y, 1 - h, c)
    recv("Az", part(x_v, across), row_dev(y, 1 - h, c))
    chunk = part(x_v, across)
    send("Ar1", chunk, chunk, row_dev(yr, h, c))
    send("Al1", chunk, chunk, row_dev(yl, h, c))
    send("Ao1", chunk, chunk, row_dev(yo, h, c))
    share("z", across)
    opp = row_of(yo, h, c)
    recv("Arr", part(x_v, opp, 0, 2), row_dev(yl, h, c))
    share("o0a", opp, 0, 2)
    recv("All", part(x_v, opp, 2, 4), row_dev(yr, h, c))
    share("o0b", opp, 2, 4)
    far = [row_of(yl, 1 - h, c), row_of(yr, 1 - h, c), row_of(yo, 1 - h, c)]
    recv("Ar1", part(x_v, far[0]), row_dev(yl, h, c))
    share("l1", far[0])
    recv("Al1", part(x_v, far[1]), row_dev(yr, h, c))
    share("r1", far[1])
    recv("Ao1", part(x_v, far[2]), row_dev(yo, h, c))
    share("o1", far[2])

    def shared(name, chunk, lo=0, hi=4):
        recv("S" + name, part(x_v, chunk, lo, hi), sibling)

    load_f.wait()
    load_t.wait()
    load_a.wait()
    d = 1 - c
    recv("As", part(x_v, row_of(y, h, d)), sibling)
    shared("l0", row_of(yl, h, d))
    shared("r0", row_of(yr, h, d))
    shared("z", row_of(y, 1 - h, d))
    shared("o0a", row_of(yo, h, d), 0, 2)
    shared("o0b", row_of(yo, h, d), 2, 4)
    shared("l1", row_of(yl, 1 - h, d))
    shared("r1", row_of(yr, 1 - h, d))
    shared("o1", row_of(yo, 1 - h, d))

    def spmm(base, source, adjacency_right):
        def step(k, total):
            block = a_v[tab[base, k]]
            other = source[tab[base + 1, k]]
            if adjacency_right:
                product = jnp.dot(other, block, preferred_element_type=F32)
            else:
                product = jnp.dot(block, other, preferred_element_type=F32)
            total = jnp.where(tab[base + 2, k] != 0, total, 0.0) + product
            s_v[k] = total
            return total

        lax.fori_loop(0, SLOTS, step, jnp.zeros((BLK, BLK), F32), unroll=UNROLL)

    spmm(0, x_v, False)

    def partial(chunk, b):
        return s_v[tab[3, chunk * 4 + b]]

    def each(lo, hi, body):
        def step(b, carry):
            body(b)
            return carry

        lax.fori_loop(lo, hi, step, 0)

    def fill(chunk, lo, hi):
        def body(b):
            p_v[chunk * 4 + b] = partial(chunk, b).astype(BF)

        each(lo, hi, body)

    zj = [(z + 1 + j) % 4 for j in range(4)]
    to_r, to_l = col_dev(xr, z), col_dev(xl, z)

    def relay(j):
        chunk = xo * 4 + zj[j]
        fill(chunk, 0, 4)
        send(f"Brr{j}", part(p_v, chunk, 0, 2), rl.at[j], to_r)
        send(f"Brl{j}", part(p_v, chunk, 2, 4), rr.at[j], to_l)

    def raw(j):
        chunk = xr * 4 + zj[j]
        fill(chunk, 2, 4)
        send(f"Bwr{j}", part(p_v, chunk, 2, 4), rxl.at[j, pl.ds(2, 2)], to_r)
        chunk = xl * 4 + zj[j]
        fill(chunk, 0, 2)
        send(f"Bwl{j}", part(p_v, chunk, 0, 2), rxr.at[j, pl.ds(0, 2)], to_l)

    def summed(j):
        chunk_r = xr * 4 + zj[j]
        recv(f"Brr{j}", rl.at[j], to_l)

        def body_r(b):
            p_v[chunk_r * 4 + b] = (partial(chunk_r, b) + rl[j, b].astype(F32)).astype(BF)

        each(0, 2, body_r)
        send(f"Bsr{j}", part(p_v, chunk_r, 0, 2), rxl.at[j, pl.ds(0, 2)], to_r)
        chunk_l = xl * 4 + zj[j]
        recv(f"Brl{j}", rr.at[j], to_r)

        def body_l(b):
            p_v[chunk_l * 4 + 2 + b] = (partial(chunk_l, b + 2) + rr[j, b].astype(F32)).astype(BF)

        each(0, 2, body_l)
        send(f"Bsl{j}", part(p_v, chunk_l, 2, 4), rxr.at[j, pl.ds(2, 2)], to_l)

    def finish(j):
        recv(f"Bwr{j}", rxl.at[j, pl.ds(2, 2)], to_l)
        recv(f"Bwl{j}", rxr.at[j, pl.ds(0, 2)], to_r)
        recv(f"Bsr{j}", rxl.at[j, pl.ds(0, 2)], to_l)
        recv(f"Bsl{j}", rxr.at[j, pl.ds(2, 2)], to_r)
        chunk = x * 4 + zj[j]

        def body(b):
            total = partial(chunk, b) + rxl[j, b].astype(F32) + rxr[j, b].astype(F32)
            if j < 3:
                zs[j, b] = total.astype(BF)
            else:
                tz[b] = total

        each(0, 4, body)
        if j < 3:
            send(f"Bz{j}", zs.at[j], rz.at[j], col_dev(x, zj[j]))

    relay(0)
    raw(0)
    relay(1)
    for j in range(4):
        summed(j)
        if j < 3:
            raw(j + 1)
        if j < 2:
            relay(j + 2)
        if j > 0:
            finish(j - 1)
    finish(3)
    load_w.wait()
    load_c.wait()
    for j in range(3):
        recv(f"Bz{j}", rz.at[j], col_dev(x, (z + 3 - j) % 4))

    def layer(b):
        agg = tz[b] + rz[0, b].astype(F32) + rz[1, b].astype(F32) + rz[2, b].astype(F32)
        high = agg.astype(BF)
        low = (agg - high.astype(F32)).astype(BF)
        hi_v[b] = high
        lo_v[b] = low
        w = w_v[...]
        pre = jnp.dot(high, w, preferred_element_type=F32) + jnp.dot(low, w, preferred_element_type=F32)
        s = lax.logistic(pre)
        act_v[b] = (pre * s).astype(BF)
        grad = (cot_v[b].astype(F32) * s * (1.0 + pre * (1.0 - s))).astype(BF)
        gp_v[b] = grad
        narrow = lax.dot_general(w, grad, (((1,), (1,)), ((), ())), preferred_element_type=F32)
        g_v[col * 4 + b] = narrow.astype(BF)

    each(0, 4, layer)

    zsrc = [z, (z + 3) % 4, (z + 1) % 4, (z + 2) % 4]
    zdst = [z, (z + 1) % 4, (z + 3) % 4, (z + 2) % 4]

    def along(s):
        chunk = part(g_v, x * 4 + zsrc[s])
        send(f"Cr{s}", chunk, chunk, to_r)
        send(f"Cl{s}", chunk, chunk, to_l)

    def pass_on(s):
        chunk = xl * 4 + zsrc[s]
        recv(f"Cr{s}", part(g_v, chunk), to_l)
        send(f"Crr{s}", part(g_v, chunk, 0, 2), part(g_v, chunk, 0, 2), to_r)
        chunk = xr * 4 + zsrc[s]
        recv(f"Cl{s}", part(g_v, chunk), to_r)
        send(f"Cll{s}", part(g_v, chunk, 2, 4), part(g_v, chunk, 2, 4), to_l)

    along(0)
    mine = part(g_v, col)
    for s in (1, 2, 3):
        send(f"Cz{s}", mine, mine, col_dev(x, zdst[s]))
    store_a = pltpu.make_async_copy(act_v, act_out, local_sem.at[5])
    store_a.start()

    gwp[...] = jnp.zeros_like(gwp)

    def weight_term(b):
        dims = (((0,), (0,)), ((), ()))
        grad = gp_v[b]
        gwp[...] += lax.dot_general(hi_v[b], grad, dims, preferred_element_type=F32) + lax.dot_general(
            lo_v[b], grad, dims, preferred_element_type=F32
        )

    each(0, 4, weight_term)
    for k in (1, 2, 3):
        to = (x + k) % 4
        send(f"Gx{k}", gwp.at[pl.ds(pl.multiple_of(to * 32, 32), 32)], gx.at[k - 1], col_dev(to, z))

    def arrive(s):
        chunk = part(g_v, x * 4 + zsrc[s])
        recv(f"Cz{s}", chunk, col_dev(x, zsrc[s]))

    arrive(1)
    along(1)
    pass_on(0)
    for k in (1, 2, 3):
        recv(f"Gx{k}", gx.at[k - 1], col_dev((x + 4 - k) % 4, z))
    g1[...] = gwp[pl.ds(pl.multiple_of(x * 32, 32), 32), :] + gx[0] + gx[1] + gx[2]
    for k in (1, 2, 3):
        to = (z + k) % 4
        send(f"Gz{k}", g1.at[pl.ds(pl.multiple_of(to * 8, 8), 8)], gz.at[k - 1], col_dev(x, to))
    arrive(2)
    along(2)
    pass_on(1)
    for k in (1, 2, 3):
        recv(f"Gz{k}", gz.at[k - 1], col_dev(x, (z + 4 - k) % 4))
    gy[y] = g1[pl.ds(pl.multiple_of(z * 8, 8), 8), :] + gz[0] + gz[1] + gz[2]
    for k in (1, 2, 3):
        send(f"Gy{k}", gy.at[y], gy.at[y], row_dev((y + k) % 4, h, c))
    arrive(3)
    along(3)
    pass_on(2)
    for k in (1, 2, 3):
        frm = (y + 4 - k) % 4
        recv(f"Gy{k}", gy.at[frm], row_dev(frm, h, c))
    g3[...] = gy[0] + gy[1] + gy[2] + gy[3]
    send("Gc", g3, gc, sibling)
    pass_on(3)
    recv("Gc", gc, sibling)
    g4[...] = g3[...] + gc[...]
    across_dev = row_dev(y, 1 - h, c)
    send("Gh", g4, gh, across_dev)
    for s in range(4):
        chunk = xo * 4 + zsrc[s]
        recv(f"Crr{s}", part(g_v, chunk, 0, 2), to_l)
        recv(f"Cll{s}", part(g_v, chunk, 2, 4), to_r)

    spmm(4, g_v, True)

    recv("Gh", gh, across_dev)
    at = pl.multiple_of(x * 32 + z * 8, 8)
    scale = 1.0 / math.sqrt(BLK * BLOCKS * 16)
    gwf[pl.ds(at, 8), :] = (g4[...] + gh[...]) * scale
    for k in (1, 2, 3):
        piece = gwf.at[pl.ds(at, 8)]
        send(f"Gu{k}", piece, piece, col_dev(x, (z + k) % 4))

    def partial2(chunk, b):
        return s_v[tab[7, chunk * 4 + b]]

    order = [(y_, h_) for h_ in (1 - h, h) for y_ in (yo, yr, yl, y)]
    for i, (y_, h_) in enumerate(order):
        chunk = row_of(y_, h_, 1 - c)

        def body(b, chunk=chunk):
            p2_v[chunk * 4 + b] = partial2(chunk, b).astype(BF)

        each(0, 4, body)
        send(f"Es{i}", part(p2_v, chunk), sib.at[i], sibling)

    def both(i, chunk, b):
        return partial2(chunk, b) + sib[i, b].astype(F32)

    up, down = row_dev(yr, h, c), row_dev(yl, h, c)

    def chunk_of(i):
        return row_of(order[i][0], order[i][1], c)

    def store_both(i, lo, hi):
        chunk = chunk_of(i)

        def body(b):
            p2_v[chunk * 4 + b] = both(i, chunk, b).astype(BF)

        each(lo, hi, body)

    def relay2(g):
        i = 4 * g
        recv(f"Es{i}", sib.at[i], sibling)
        store_both(i, 0, 4)
        send(f"Err{g}", part(p2_v, chunk_of(i), 0, 2), rl2.at[g], up)
        send(f"Erl{g}", part(p2_v, chunk_of(i), 2, 4), rr2.at[g], down)

    def raw2(g):
        i = 4 * g + 1
        recv(f"Es{i}", sib.at[i], sibling)
        store_both(i, 2, 4)
        send(f"Ewr{g}", part(p2_v, chunk_of(i), 2, 4), rxl2.at[g, pl.ds(2, 2)], up)
        i = 4 * g + 2
        recv(f"Es{i}", sib.at[i], sibling)
        store_both(i, 0, 2)
        send(f"Ewl{g}", part(p2_v, chunk_of(i), 0, 2), rxr2.at[g, pl.ds(0, 2)], down)

    def summed2(g):
        i = 4 * g + 1
        chunk_r = chunk_of(i)
        recv(f"Err{g}", rl2.at[g], down)

        def body_r(b):
            p2_v[chunk_r * 4 + b] = (both(i, chunk_r, b) + rl2[g, b].astype(F32)).astype(BF)

        each(0, 2, body_r)
        send(f"Esr{g}", part(p2_v, chunk_r, 0, 2), rxl2.at[g, pl.ds(0, 2)], up)
        i2 = 4 * g + 2
        chunk_l = chunk_of(i2)
        recv(f"Erl{g}", rr2.at[g], up)

        def body_l(b):
            p2_v[chunk_l * 4 + 2 + b] = (both(i2, chunk_l, b + 2) + rr2[g, b].astype(F32)).astype(BF)

        each(0, 2, body_l)
        send(f"Esl{g}", part(p2_v, chunk_l, 2, 4), rxr2.at[g, pl.ds(2, 2)], down)

    def gathered2(g):
        i = 4 * g + 3
        recv(f"Es{i}", sib.at[i], sibling)
        recv(f"Ewr{g}", rxl2.at[g, pl.ds(2, 2)], down)
        recv(f"Ewl{g}", rxr2.at[g, pl.ds(0, 2)], up)
        recv(f"Esr{g}", rxl2.at[g, pl.ds(0, 2)], down)
        recv(f"Esl{g}", rxr2.at[g, pl.ds(2, 2)], up)
        chunk = chunk_of(i)

        def total(b):
            return both(i, chunk, b) + rxl2[g, b].astype(F32) + rxr2[g, b].astype(F32)

        return total

    relay2(0)
    raw2(0)
    relay2(1)
    summed2(0)
    raw2(1)
    total = gathered2(0)

    def to_across(b):
        zs2[b] = total(b).astype(BF)

    each(0, 4, to_across)
    send("Ez", zs2, rz2, across_dev)
    summed2(1)
    for k in (1, 2, 3):
        frm = (z + 4 - k) % 4
        recv(f"Gu{k}", gwf.at[pl.ds(pl.multiple_of(x * 32 + frm * 8, 8), 8)], col_dev(x, frm))
    for k in (1, 2, 3):
        piece = gwf.at[pl.ds(pl.multiple_of(x * 32, 32), 32)]
        send(f"Gv{k}", piece, piece, col_dev((x + k) % 4, z))
    total2 = gathered2(1)
    flush_before = list(pending)
    del pending[:]
    for copy in flush_before:
        copy.wait_send()
    recv("Ez", rz2, across_dev)

    def output(b):
        gi_v[b] = (total2(b) + rz2[b].astype(F32)).T.astype(BF)

    each(0, 4, output)
    store_i = pltpu.make_async_copy(gi_v, gi_out, local_sem.at[6])
    store_i.start()
    for k in (1, 2, 3):
        frm = (x + 4 - k) % 4
        recv(f"Gv{k}", gwf.at[pl.ds(pl.multiple_of(frm * 32, 32), 32)], col_dev(frm, z))
    store_w = pltpu.make_async_copy(gwf, gw_out, local_sem.at[7])
    store_w.start()
    flush()
    store_a.wait()
    store_i.wait()
    store_w.wait()


def on_device(features, weight, cotangent, adj_blocks, block_rows, block_cols, live_mask):
    hbm = pl.BlockSpec(memory_space=pl.ANY)
    vmem = pl.BlockSpec(memory_space=pltpu.VMEM)
    quad = (4, BLK, BLK)
    scratch = [
        pltpu.VMEM((SLOTS, BLK, BLK), BF),
        pltpu.VMEM((BLOCKS, BLK, BLK), BF),
        pltpu.VMEM((SLOTS + 1, BLK, BLK), F32),
        pltpu.VMEM((BLOCKS, BLK, BLK), BF),
        pltpu.VMEM((BLOCKS, BLK, BLK), BF),
        pltpu.VMEM((BLOCKS, BLK, BLK), BF),
        pltpu.VMEM((BLK, 2 * BLK), BF),
        pltpu.VMEM((4, BLK, 2 * BLK), BF),
        pltpu.VMEM((4, BLK, 2 * BLK), BF),
        pltpu.VMEM((4, BLK, 2 * BLK), BF),
        pltpu.VMEM(quad, BF),
        pltpu.VMEM(quad, BF),
        pltpu.VMEM(quad, BF),
        pltpu.VMEM((4, 2, BLK, BLK), BF),
        pltpu.VMEM((4, 2, BLK, BLK), BF),
        pltpu.VMEM((4,) + quad, BF),
        pltpu.VMEM((4,) + quad, BF),
        pltpu.VMEM((3,) + quad, BF),
        pltpu.VMEM((3,) + quad, BF),
        pltpu.VMEM(quad, F32),
        pltpu.VMEM((8,) + quad, BF),
        pltpu.VMEM((2, 2, BLK, BLK), BF),
        pltpu.VMEM((2, 2, BLK, BLK), BF),
        pltpu.VMEM((2,) + quad, BF),
        pltpu.VMEM((2,) + quad, BF),
        pltpu.VMEM(quad, BF),
        pltpu.VMEM(quad, BF),
        pltpu.VMEM((BLK, 2 * BLK), F32),
        pltpu.VMEM((3, 32, 2 * BLK), F32),
        pltpu.VMEM((32, 2 * BLK), F32),
        pltpu.VMEM((3, 8, 2 * BLK), F32),
        pltpu.VMEM((4, 8, 2 * BLK), F32),
        pltpu.VMEM((8, 2 * BLK), F32),
        pltpu.VMEM((8, 2 * BLK), F32),
        pltpu.VMEM((8, 2 * BLK), F32),
        pltpu.VMEM((8, 2 * BLK), F32),
        pltpu.VMEM((BLK, 2 * BLK), F32),
        pltpu.VMEM((8, SLOTS), jnp.int32),
        pltpu.SMEM((8, SLOTS), jnp.int32),
        pltpu.SemaphoreType.DMA((128,)),
        pltpu.SemaphoreType.DMA((128,)),
        pltpu.SemaphoreType.DMA((8,)),
    ]
    act, gi, gw = pl.pallas_call(
        kernel,
        out_shape=(
            jax.ShapeDtypeStruct((4, BLK, 2 * BLK), BF),
            jax.ShapeDtypeStruct(quad, BF),
            jax.ShapeDtypeStruct((BLK, 2 * BLK), F32),
        ),
        in_specs=[hbm, hbm, hbm, hbm, vmem, vmem, vmem],
        out_specs=(hbm, hbm, hbm),
        scratch_shapes=scratch,
        compiler_params=pltpu.CompilerParams(
            collective_id=0, has_side_effects=True, vmem_limit_bytes=60 << 20
        ),
        cost_estimate=pl.CostEstimate(flops=2 << 30, bytes_accessed=12 << 20, transcendentals=1 << 17),
        name="graph_layer",
    )(
        features.reshape(quad),
        weight,
        cotangent.reshape(4, BLK, 2 * BLK),
        adj_blocks.reshape(SLOTS, BLK, BLK),
        block_rows.reshape(1, SLOTS),
        block_cols.reshape(1, SLOTS),
        live_mask.reshape(1, SLOTS),
    )
    return act.reshape(4 * BLK, 2 * BLK), gi.reshape(4 * BLK, BLK), gw


def solution(mesh):
    in_specs = (
        P(("col", "row"), None),
        P(),
        P(("row", "col"), None),
        P("row", "col", None, None, None),
        P("row", "col", None),
        P("row", "col", None),
        P("row", "col", None),
    )
    out_specs = (P(("row", "col"), None), P(("col", "row"), None), P())
    return jax.shard_map(
        on_device, mesh=mesh, in_specs=in_specs, out_specs=out_specs, check_vma=False
    )
```

time: 889 us -> 110 us (0.12)
  waiting for transfers between devices: 635 us -> 0 us
  other arithmetic: 134 us -> 0 us
  Pallas kernels: 0 us -> 104 us
  matrix products: 53.5 us -> 0 us
  local copies, waits for them, and re-layouts: 49.4 us -> 4.8 us
  between operations: 13.8 us -> 0.64 us
    psum x1 -> x0, waiting for transfers between devices: 239 us -> none  [on_device(): lax.psum(local_term, ('row', 'col')) * (1.0 / math.sqrt(nodes))]
    reduce_scatter x2 -> x0, waiting for transfers between devices: 235 us -> none  [the longest x1 140 us: on_device(): lax.psum_scatter(backward, 'row', scatter_dimension=0, tiled=True)]
    all_gather x2 -> x0, waiting for transfers between devices: 160 us -> none  [the longest x1 90.4 us: on_device(): spread_rows = lax.all_gather(grad_pre, 'col', axis=0, tiled=True)]
    scatter-add x8 -> x0, other arithmetic: 132 us -> none  [one_turn(): return total.at[places].add(product)]
    pallas_call x0 -> x1, Pallas kernels: none -> 104 us  [on_device(): pl.pallas_call(kernel, out_shape=(jax.ShapeDtypeStruct((4, BLK, 2 * BLK),...]
    dot_general x11 -> x0, matrix products: 53.5 us -> none  [the longest x8 46.8 us: one_turn(): jnp.einsum(einsum_form, tile_vals, gathered, preferred_element_type=jnp.f...]
    gather x8 -> x0, local copies, waits for them, and re-layouts: 29.9 us -> none  [one_turn(): gathered = jnp.take(blocked, picks, axis=0)]
  transfers between devices with their start and end apart: 5 -> 0, of which waited for: 5 -> 0; matrix products, arithmetic and copies ran while one was open for 2% -> 0% of each run, Pallas kernels for 0% -> 0%
where the time goes in v1:
time: 110 us
  Pallas kernels  104 us (95%)
  local copies, waits for them, and re-layouts  4.8 us (4%)
    pallas_call x1, Pallas kernels, on_device(): pl.pallas_call(kernel, out_shape=(jax.ShapeDtypeStruct((4, BLK, 2 * BLK),...  104 us
    unnamed x3, local copies, waits for them, and re-layouts  4.8 us

profile of v1, /device:TPU:1, one launch (start us, length us, event | category | flops | bytes accessed | tf_op | source)
XLA Modules:
  0.0 109.6 jit_solution(7270004510144493370)
XLA Ops:
  0.6 104.2 %graph_layer.1 = (bf16[4,128,256]{2,1,0:T(8,128)(2,1)}, bf16[4,128,128]{2,1,0:T(8,128)(2,1)}, f32[128,256]{1,0:T(8,128)}) custom-call(bf16[4,128,128]{2,1,0:T(8,128)(2,1)} %bitcast.11, bf16[128,256]{1,0:T(8,128)(2,1)} %weight.1, bf16[4,128,256]{2,1,0:T(8,128)(2,1)} %bitcast.9, bf16[256,128,128]{2,1,0:T(8,128)(2,1)} %bitcast.8, s32[1,256]{1,0:T(1,128)} %bitcast.13, ...), custom_call_target="tpu_custom_call" | custom-call | flops 2147483648 | bytes 12582912 | tf_op jit(solution)/shard_map/graph_layer/pallas_call | solution.py:557
  104.8 1.7 %copy.13 = bf16[512,256]{1,0:T(8,128)(2,1)} copy(bf16[512,256]{1,0:T(8,128)(2,1)} %bitcast.10) | data formatting | bytes 524288
  106.5 1.6 %copy.14 = bf16[512,128]{1,0:T(8,128)(2,1)} copy(bf16[512,128]{1,0:T(8,128)(2,1)} %bitcast.12) | data formatting | bytes 262144
  108.0 1.6 %copy.15 = f32[128,256]{1,0:T(8,128)} copy(f32[128,256]{1,0:T(8,128)} %get-tuple-element.14) | data formatting | bytes 262144

commit v2 on v1

v2 whole, which is shorter than its diff:
```python
import functools
import math

import jax
import jax.numpy as jnp
from jax import lax
from jax.experimental import pallas as pl
from jax.experimental.pallas import tpu as pltpu
from jax.sharding import PartitionSpec as P

MESH = pl.DeviceIdType.MESH
BF = jnp.bfloat16
F32 = jnp.float32
BLK = 128
SLOTS = 256
BLOCKS = 64
HALF = 64
STRAIGHT = ((0, 3), (1, 2), (1, 3))
UNROLL = 64


def slot_tables(put, pick, live):
    shape = (SLOTS, SLOTS)
    put_lane = jnp.broadcast_to(jnp.where(live != 0, put, BLOCKS), shape)
    put_sub = put_lane.T
    pick_sub = jnp.broadcast_to(pick, shape).T
    sub = lax.broadcasted_iota(jnp.int32, shape, 0)
    lane = lax.broadcasted_iota(jnp.int32, shape, 1)

    def count(mask, axis):
        return jnp.sum(mask.astype(jnp.int32), axis=axis, keepdims=True)

    rank = count(put_lane * SLOTS + lane < put_sub * SLOTS + sub, 1)
    chosen = rank == lane
    continues = count((put_lane == put_sub) & (lane < sub), 1) > 0
    order = jnp.sum(jnp.where(chosen, sub, 0), axis=0, keepdims=True)
    source = jnp.sum(jnp.where(chosen, pick_sub, 0), axis=0, keepdims=True)
    follow = count(chosen & continues, 0)
    held = count(put_sub == lane, 0)
    upto = count(put_sub <= lane, 0)
    last = jnp.where(held > 0, upto - 1, SLOTS)
    return order, source, follow, last


def kernel(
    feat, weight, cot, adj, rows, cols, live,
    act_out, gi_out, gw_out,
    a_v, at_v, f_v, x_0, x_1, s_v, p_v, g_0, g_1, p2_v, w_v, cot_v, act_v, gp_v, hi_v, lo_v, gi_v,
    rl, rr, rxl, rxr, zs, rz, tz,
    sib, rl2, rr2, rxl2, rxr2, zs2, rz2,
    gwp, gx, g1, gz, gy, g3, gc, g4, gh, gwf,
    tab_v, tab, send_sem, recv_sem, local_sem,
):
    row = lax.axis_index("row")
    col = lax.axis_index("col")
    y, h, c = row // 4, (row // 2) % 2, row % 2
    x, z = col // 4, col % 4
    xr, xo, xl = (x + 1) % 4, (x + 2) % 4, (x + 3) % 4
    yr, yo, yl = (y + 1) % 4, (y + 2) % 4, (y + 3) % 4

    def col_dev(x_, z_):
        return (row, x_ * 4 + z_)

    def row_of(y_, h_, c_):
        return y_ * 4 + h_ * 2 + c_

    def row_dev(y_, h_, c_):
        return (row_of(y_, h_, c_), col)

    x_v, g_v = (x_0, x_1), (g_0, g_1)
    to_r, to_l, to_o = col_dev(xr, z), col_dev(xl, z), col_dev(xo, z)
    up, down, over = row_dev(yr, h, c), row_dev(yl, h, c), row_dev(yo, h, c)
    across_dev, sibling = row_dev(y, 1 - h, c), row_dev(y, h, 1 - c)

    peers = [to_r, col_dev(xo, z), to_l]
    peers += [col_dev(x, (z + d) % 4) for d in (1, 2, 3)]
    peers += [up, over, down, across_dev, sibling]
    barrier = pltpu.get_barrier_semaphore()
    for peer in peers:
        pl.semaphore_signal(barrier, inc=1, device_id=peer, device_id_type=MESH)

    names = {}
    pending = []

    def number(name):
        return names.setdefault(name, len(names))

    def send(name, src, dst, device):
        k = number(name)
        copy = pltpu.make_async_remote_copy(
            src_ref=src, dst_ref=dst, send_sem=send_sem.at[k], recv_sem=recv_sem.at[k],
            device_id=device, device_id_type=MESH,
        )
        copy.start()
        pending.append(copy)

    def recv(name, dst, device):
        k = number(name)
        pltpu.make_async_remote_copy(
            src_ref=dst, dst_ref=dst, send_sem=send_sem.at[k], recv_sem=recv_sem.at[k],
            device_id=device, device_id_type=MESH,
        ).wait_recv()

    def flush(copies):
        for copy in copies:
            copy.wait_send()

    def taken():
        copies = list(pending)
        del pending[:]
        return copies

    def each(lo, hi, body):
        def step(b, carry):
            body(b)
            return carry

        lax.fori_loop(lo, hi, step, 0, unroll=hi - lo)

    load_f = pltpu.make_async_copy(feat, f_v, local_sem.at[3])
    load_f.start()
    load_a = pltpu.make_async_copy(adj, a_v, local_sem.at[0])
    load_a.start()
    load_w = pltpu.make_async_copy(weight, w_v, local_sem.at[1])
    load_w.start()
    load_c = pltpu.make_async_copy(cot, cot_v, local_sem.at[2])
    load_c.start()

    def part(ref, f, chunk, lo=0, hi=4):
        at = pl.ds(chunk * 4 + lo, hi - lo)
        return ref[f].at[at] if isinstance(ref, tuple) else ref.at[f, at]

    load_f.wait()

    def turn(b):
        turned = f_v[b].T
        x_0[row * 4 + b] = turned[:HALF]
        x_1[row * 4 + b] = turned[HALF:]

    each(0, 4, turn)
    pl.semaphore_wait(barrier, len(peers))

    def begin(f):
        own = part(x_v, f, row)
        send(f"Az{f}", own, own, across_dev)
        send(f"Ar{f}", own, own, up)
        send(f"Al{f}", own, own, down)
        send(f"As{f}", own, own, sibling)

    begin(0)
    table = slot_tables(rows[...], cols[...], live[...])
    for k in range(4):
        tab_v[k : k + 1, :] = table[k]
    table = slot_tables(cols[...], rows[...], live[...])
    for k in range(4):
        tab_v[k + 4 : k + 5, :] = table[k]
    load_t = pltpu.make_async_copy(tab_v, tab, local_sem.at[4])
    load_t.start()
    for f in range(2):
        s_v[f, SLOTS] = jnp.zeros((HALF, BLK), F32)

    def share(name, f, chunk, lo=0, hi=4):
        send("S" + name, part(x_v, f, chunk, lo, hi), part(x_v, f, chunk, lo, hi), sibling)

    left, right, opp = row_of(yl, h, c), row_of(yr, h, c), row_of(yo, h, c)
    across = row_of(y, 1 - h, c)
    far = [row_of(yl, 1 - h, c), row_of(yr, 1 - h, c), row_of(yo, 1 - h, c)]

    def beside(f):
        recv(f"Ar{f}", part(x_v, f, left), down)
        send(f"Arr{f}", part(x_v, f, left, 0, 2), part(x_v, f, left, 0, 2), up)
        share(f"l{f}", f, left)
        recv(f"Al{f}", part(x_v, f, right), up)
        send(f"All{f}", part(x_v, f, right, 2, 4), part(x_v, f, right, 2, 4), down)
        share(f"r{f}", f, right)

    def crossed(f):
        piece = part(x_v, f, across)
        recv(f"Az{f}", piece, across_dev)
        send(f"Afr{f}", piece, piece, up)
        send(f"Afl{f}", piece, piece, down)
        send(f"Afo{f}", piece, piece, over)
        share(f"z{f}", f, across)

    def opposite(f):
        recv(f"Arr{f}", part(x_v, f, opp, 0, 2), down)
        share(f"oa{f}", f, opp, 0, 2)
        recv(f"All{f}", part(x_v, f, opp, 2, 4), up)
        share(f"ob{f}", f, opp, 2, 4)

    def remote(f):
        recv(f"Afr{f}", part(x_v, f, far[0]), down)
        share(f"fl{f}", f, far[0])
        recv(f"Afl{f}", part(x_v, f, far[1]), up)
        share(f"fr{f}", f, far[1])
        recv(f"Afo{f}", part(x_v, f, far[2]), over)
        share(f"fo{f}", f, far[2])

    def shared(f):
        d = 1 - c

        def take(name, chunk, lo=0, hi=4):
            recv(name, part(x_v, f, chunk, lo, hi), sibling)

        take(f"As{f}", row_of(y, h, d))
        take(f"Sl{f}", row_of(yl, h, d))
        take(f"Sr{f}", row_of(yr, h, d))
        take(f"Sz{f}", row_of(y, 1 - h, d))
        take(f"Soa{f}", row_of(yo, h, d), 0, 2)
        take(f"Sob{f}", row_of(yo, h, d), 2, 4)
        take(f"Sfl{f}", row_of(yl, 1 - h, d))
        take(f"Sfr{f}", row_of(yr, 1 - h, d))
        take(f"Sfo{f}", row_of(yo, 1 - h, d))

    def turn_blocks(n):
        def step(k, carry):
            at_v[k] = a_v[k].T
            return carry

        lax.fori_loop(64 * n, 64 * n + 64, step, 0, unroll=16)

    def spmm(f, base, source, blocks):
        def step(k, total):
            block = blocks[tab[base, k]]
            other = source[f][tab[base + 1, k]]
            product = jnp.dot(other, block, preferred_element_type=F32)
            total = jnp.where(tab[base + 2, k] != 0, total, 0.0) + product
            s_v[f, k] = total
            return total

        held = [jnp.zeros((HALF, BLK), F32)]

        def quarter(n):
            held[0] = lax.fori_loop(64 * n, 64 * n + 64, step, held[0], unroll=64)

        return quarter

    beside(0)
    begin(1)
    crossed(0)
    load_a.wait()
    turn_blocks(0)
    opposite(0)
    beside(1)
    turn_blocks(1)
    crossed(1)
    turn_blocks(2)
    remote(0)
    turn_blocks(3)
    opposite(1)
    load_t.wait()
    shared(0)
    quarter = spmm(0, 0, x_v, at_v)
    for n in range(4):
        quarter(n)

    def partial(f, chunk, b):
        return s_v[f, tab[3, chunk * 4 + b]]

    def fill(f, chunk, lo, hi):
        def body(b):
            p_v[f, chunk * 4 + b] = partial(f, chunk, b).astype(BF)

        each(lo, hi, body)

    zj = [(z + 1 + j) % 4 for j in range(4)]

    def pair(ref, f, j, lo):
        return ref.at[f, j, pl.ds(lo, 2)]

    def relay(f, j):
        chunk = xo * 4 + zj[j]
        fill(f, chunk, 0, 4)
        send(f"Brr{f}{j}", part(p_v, f, chunk, 0, 2), rl.at[f, j], to_r)
        send(f"Brl{f}{j}", part(p_v, f, chunk, 2, 4), rr.at[f, j], to_l)

    def raw(f, j):
        chunk = xr * 4 + zj[j]
        fill(f, chunk, 2, 4)
        send(f"Bwr{f}{j}", part(p_v, f, chunk, 2, 4), pair(rxl, f, j, 2), to_r)
        chunk = xl * 4 + zj[j]
        fill(f, chunk, 0, 2)
        send(f"Bwl{f}{j}", part(p_v, f, chunk, 0, 2), pair(rxr, f, j, 0), to_l)

    def summed(f, j):
        chunk_r = xr * 4 + zj[j]
        recv(f"Brr{f}{j}", rl.at[f, j], to_l)

        def body_r(b):
            p_v[f, chunk_r * 4 + b] = (partial(f, chunk_r, b) + rl[f, j, b].astype(F32)).astype(BF)

        each(0, 2, body_r)
        send(f"Bsr{f}{j}", part(p_v, f, chunk_r, 0, 2), pair(rxl, f, j, 0), to_r)
        chunk_l = xl * 4 + zj[j]
        recv(f"Brl{f}{j}", rr.at[f, j], to_r)

        def body_l(b):
            p_v[f, chunk_l * 4 + 2 + b] = (
                partial(f, chunk_l, b + 2) + rr[f, j, b].astype(F32)
            ).astype(BF)

        each(0, 2, body_l)
        send(f"Bsl{f}{j}", part(p_v, f, chunk_l, 2, 4), pair(rxr, f, j, 2), to_l)

    def finish(f, j):
        recv(f"Bwr{f}{j}", pair(rxl, f, j, 2), to_l)
        recv(f"Bwl{f}{j}", pair(rxr, f, j, 0), to_r)
        recv(f"Bsr{f}{j}", pair(rxl, f, j, 0), to_l)
        recv(f"Bsl{f}{j}", pair(rxr, f, j, 2), to_r)
        chunk = x * 4 + zj[j]

        def body(b):
            total = partial(f, chunk, b) + rxl[f, j, b].astype(F32) + rxr[f, j, b].astype(F32)
            if j < 3:
                zs[f, j, b] = total.astype(BF)
            else:
                tz[f, b] = total

        each(0, 4, body)
        if j < 3:
            send(f"Bz{f}{j}", zs.at[f, j], rz.at[f, j], col_dev(x, zj[j]))

    quarter = spmm(1, 0, x_v, at_v)
    relay(0, 0)
    raw(0, 0)
    relay(0, 1)
    remote(1)
    summed(0, 0)
    raw(0, 1)
    relay(0, 2)
    shared(1)
    quarter(0)
    summed(0, 1)
    raw(0, 2)
    relay(0, 3)
    quarter(1)
    finish(0, 0)
    raw(0, 3)
    quarter(2)
    summed(0, 2)
    finish(0, 1)
    quarter(3)
    relay(1, 0)
    summed(0, 3)
    raw(1, 0)
    relay(1, 1)
    finish(0, 2)
    done = taken()
    summed(1, 0)
    raw(1, 1)
    relay(1, 2)
    finish(0, 3)
    summed(1, 1)
    raw(1, 2)
    relay(1, 3)
    finish(1, 0)
    summed(1, 2)
    raw(1, 3)
    finish(1, 1)
    summed(1, 3)
    flush(done)
    finish(1, 2)
    load_w.wait()
    load_c.wait()
    finish(1, 3)
    for f in range(2):
        for j in range(3):
            recv(f"Bz{f}{j}", rz.at[f, j], col_dev(x, (z + 3 - j) % 4))

    def layer(b):
        agg = jnp.concatenate(
            [
                tz[f, b] + rz[f, 0, b].astype(F32) + rz[f, 1, b].astype(F32) + rz[f, 2, b].astype(F32)
                for f in range(2)
            ],
            axis=0,
        ).T
        high = agg.astype(BF)
        low = (agg - high.astype(F32)).astype(BF)
        hi_v[b] = high
        lo_v[b] = low
        w = w_v[...]
        pre = jnp.dot(high, w, preferred_element_type=F32) + jnp.dot(low, w, preferred_element_type=F32)
        s = lax.logistic(pre)
        act_v[b] = (pre * s).astype(BF)
        grad = (cot_v[b].astype(F32) * s * (1.0 + pre * (1.0 - s))).astype(BF)
        gp_v[b] = grad
        narrow = lax.dot_general(w, grad, (((1,), (1,)), ((), ())), preferred_element_type=F32)
        narrow = narrow.astype(BF)
        g_0[col * 4 + b] = narrow[:HALF]
        g_1[col * 4 + b] = narrow[HALF:]

    each(0, 4, layer)

    zsrc = [z, (z + 3) % 4, (z + 1) % 4, (z + 2) % 4]
    zdst = [z, (z + 1) % 4, (z + 3) % 4, (z + 2) % 4]

    def along(f, s):
        chunk = part(g_v, f, x * 4 + zsrc[s])
        if s > 0:
            recv(f"Cz{f}{s}", chunk, col_dev(x, zsrc[s]))
        send(f"Cr{f}{s}", chunk, chunk, to_r)
        send(f"Cl{f}{s}", chunk, chunk, to_l)
        if (f, s) in STRAIGHT:
            send(f"Co{f}{s}", chunk, chunk, to_o)

    def pass_on(f, s):
        chunk = xl * 4 + zsrc[s]
        recv(f"Cr{f}{s}", part(g_v, f, chunk), to_l)
        if (f, s) not in STRAIGHT:
            send(f"Crr{f}{s}", part(g_v, f, chunk, 0, 2), part(g_v, f, chunk, 0, 2), to_r)
        chunk = xr * 4 + zsrc[s]
        recv(f"Cl{f}{s}", part(g_v, f, chunk), to_r)
        if (f, s) not in STRAIGHT:
            send(f"Cll{f}{s}", part(g_v, f, chunk, 2, 4), part(g_v, f, chunk, 2, 4), to_l)

    def passed(f):
        for s in range(4):
            chunk = xo * 4 + zsrc[s]
            if (f, s) in STRAIGHT:
                recv(f"Co{f}{s}", part(g_v, f, chunk), to_o)
            else:
                recv(f"Crr{f}{s}", part(g_v, f, chunk, 0, 2), to_l)
                recv(f"Cll{f}{s}", part(g_v, f, chunk, 2, 4), to_r)

    def beyond(f, s):
        mine = part(g_v, f, col)
        send(f"Cz{f}{s}", mine, mine, col_dev(x, zdst[s]))

    along(0, 0)
    beyond(0, 1)
    beyond(0, 2)
    along(1, 0)
    store_a = pltpu.make_async_copy(act_v, act_out, local_sem.at[5])
    store_a.start()

    gwp[...] = jnp.zeros_like(gwp)

    def weight_term(b):
        dims = (((0,), (0,)), ((), ()))
        grad = gp_v[b]
        gwp[...] += lax.dot_general(hi_v[b], grad, dims, preferred_element_type=F32) + lax.dot_general(
            lo_v[b], grad, dims, preferred_element_type=F32
        )

    each(0, 4, weight_term)
    for k in (1, 2, 3):
        to = (x + k) % 4
        send(f"Gx{k}", gwp.at[pl.ds(pl.multiple_of(to * 32, 32), 32)], gx.at[k - 1], col_dev(to, z))

    along(0, 1)
    beyond(0, 3)
    along(0, 2)
    beyond(1, 1)
    beyond(1, 2)
    pass_on(0, 0)
    for k in (1, 2, 3):
        recv(f"Gx{k}", gx.at[k - 1], col_dev((x + 4 - k) % 4, z))
    g1[...] = gwp[pl.ds(pl.multiple_of(x * 32, 32), 32), :] + gx[0] + gx[1] + gx[2]
    for k in (1, 2, 3):
        to = (z + k) % 4
        send(f"Gz{k}", g1.at[pl.ds(pl.multiple_of(to * 8, 8), 8)], gz.at[k - 1], col_dev(x, to))
    along(0, 3)
    pass_on(0, 1)
    along(1, 1)
    beyond(1, 3)
    pass_on(0, 2)
    along(1, 2)
    pass_on(1, 0)
    for k in (1, 2, 3):
        recv(f"Gz{k}", gz.at[k - 1], col_dev(x, (z + 4 - k) % 4))
    gy[y] = g1[pl.ds(pl.multiple_of(z * 8, 8), 8), :] + gz[0] + gz[1] + gz[2]
    for k in (1, 2, 3):
        send(f"Gy{k}", gy.at[y], gy.at[y], row_dev((y + k) % 4, h, c))
    pass_on(0, 3)
    along(1, 3)
    passed(0)

    quarter = spmm(0, 4, g_v, a_v)
    quarter(0)
    pass_on(1, 1)
    quarter(1)
    pass_on(1, 2)
    quarter(2)
    quarter(3)
    pass_on(1, 3)

    def partial2(f, chunk, b):
        return s_v[f, tab[7, chunk * 4 + b]]

    order = [(y_, h_) for h_ in (1 - h, h) for y_ in (yo, yr, yl, y)]

    def halve(f, i):
        chunk = row_of(order[i][0], order[i][1], 1 - c)

        def body(b):
            p2_v[f, chunk * 4 + b] = partial2(f, chunk, b).astype(BF)

        each(0, 4, body)
        send(f"Es{f}{i}", part(p2_v, f, chunk), sib.at[f, i], sibling)

    def halved(f, i):
        recv(f"Es{f}{i}", sib.at[f, i], sibling)

    def chunk_of(i):
        return row_of(order[i][0], order[i][1], c)

    def both(f, i, b):
        return partial2(f, chunk_of(i), b) + sib[f, i, b].astype(F32)

    def emit(name, f, i, lo, value, to, device):
        chunk = chunk_of(i)

        def body(b):
            p2_v[f, chunk * 4 + lo + b] = value(b).astype(BF)

        each(0, 2, body)
        send(name, part(p2_v, f, chunk, lo, lo + 2), to, device)

    def relay2(f, g):
        i = 4 * g
        halved(f, i)
        emit(f"Err{f}{g}", f, i, 0, lambda b: both(f, i, b), rl2.at[f, g], up)
        emit(f"Erl{f}{g}", f, i, 2, lambda b: both(f, i, b + 2), rr2.at[f, g], down)

    def raw2(f, g):
        i = 4 * g + 1
        halved(f, i)
        emit(f"Ewr{f}{g}", f, i, 2, lambda b: both(f, i, b + 2), pair(rxl2, f, g, 2), up)
        k = 4 * g + 2
        halved(f, k)
        emit(f"Ewl{f}{g}", f, k, 0, lambda b: both(f, k, b), pair(rxr2, f, g, 0), down)

    def summed2(f, g):
        i = 4 * g + 1
        recv(f"Err{f}{g}", rl2.at[f, g], down)
        emit(
            f"Esr{f}{g}", f, i, 0, lambda b: both(f, i, b) + rl2[f, g, b].astype(F32),
            pair(rxl2, f, g, 0), up,
        )
        k = 4 * g + 2
        recv(f"Erl{f}{g}", rr2.at[f, g], up)
        emit(
            f"Esl{f}{g}", f, k, 2, lambda b: both(f, k, b + 2) + rr2[f, g, b].astype(F32),
            pair(rxr2, f, g, 2), down,
        )

    def gathered2(f, g):
        halved(f, 4 * g + 3)
        recv(f"Ewr{f}{g}", pair(rxl2, f, g, 2), down)
        recv(f"Ewl{f}{g}", pair(rxr2, f, g, 0), up)
        recv(f"Esr{f}{g}", pair(rxl2, f, g, 0), down)
        recv(f"Esl{f}{g}", pair(rxr2, f, g, 2), up)

    def total2(f, g, b):
        return both(f, 4 * g + 3, b) + rxl2[f, g, b].astype(F32) + rxr2[f, g, b].astype(F32)

    def cross(f):
        gathered2(f, 0)

        def body(b):
            zs2[f, b] = total2(f, 0, b).astype(BF)

        each(0, 4, body)
        send(f"Ez{f}", zs2.at[f], rz2.at[f], across_dev)

    for i in range(8):
        halve(0, i)
    relay2(0, 0)
    raw2(0, 0)
    for k in (1, 2, 3):
        frm = (y + 4 - k) % 4
        recv(f"Gy{k}", gy.at[frm], row_dev(frm, h, c))
    g3[...] = gy[0] + gy[1] + gy[2] + gy[3]
    send("Gc", g3, gc, sibling)
    relay2(0, 1)
    passed(1)

    quarter = spmm(1, 4, g_v, a_v)
    quarter(0)
    summed2(0, 0)
    quarter(1)
    raw2(0, 1)
    quarter(2)
    recv("Gc", gc, sibling)
    g4[...] = g3[...] + gc[...]
    send("Gh", g4, gh, across_dev)
    quarter(3)

    for i in range(3):
        halve(1, i)
    cross(0)
    relay2(1, 0)
    for i in range(3, 7):
        halve(1, i)
    raw2(1, 0)
    summed2(0, 1)
    relay2(1, 1)
    halve(1, 7)
    recv("Gh", gh, across_dev)
    at = pl.multiple_of(x * 32 + z * 8, 8)
    scale = 1.0 / math.sqrt(BLK * BLOCKS * 16)
    gwf[pl.ds(at, 8), :] = (g4[...] + gh[...]) * scale
    for k in (1, 2, 3):
        piece = gwf.at[pl.ds(at, 8)]
        send(f"Gu{k}", piece, piece, col_dev(x, (z + k) % 4))
    done = taken()
    summed2(1, 0)
    raw2(1, 1)
    gathered2(0, 1)
    cross(1)
    summed2(1, 1)
    for k in (1, 2, 3):
        frm = (z + 4 - k) % 4
        recv(f"Gu{k}", gwf.at[pl.ds(pl.multiple_of(x * 32 + frm * 8, 8), 8)], col_dev(x, frm))
    for k in (1, 2, 3):
        piece = gwf.at[pl.ds(pl.multiple_of(x * 32, 32), 32)]
        send(f"Gv{k}", piece, piece, col_dev((x + k) % 4, z))
    flush(done)
    gathered2(1, 1)
    for f in range(2):
        recv(f"Ez{f}", rz2.at[f], across_dev)

    def output(b):
        total = [total2(f, 1, b) + rz2[f, b].astype(F32) for f in range(2)]
        gi_v[b] = jnp.concatenate(total, axis=0).T.astype(BF)

    each(0, 4, output)
    store_i = pltpu.make_async_copy(gi_v, gi_out, local_sem.at[6])
    store_i.start()
    for k in (1, 2, 3):
        frm = (x + 4 - k) % 4
        recv(f"Gv{k}", gwf.at[pl.ds(pl.multiple_of(frm * 32, 32), 32)], col_dev(frm, z))
    store_w = pltpu.make_async_copy(gwf, gw_out, local_sem.at[7])
    store_w.start()
    flush(taken())
    store_a.wait()
    store_i.wait()
    store_w.wait()


def leave(act, gi, gw, act_out, gi_out, gw_out, sem):
    copies = [
        pltpu.make_async_copy(src, dst, sem.at[k])
        for k, (src, dst) in enumerate(((act, act_out), (gi, gi_out), (gw, gw_out)))
    ]
    for copy in copies:
        copy.start()
    for copy in copies:
        copy.wait()


def on_device(features, weight, cotangent, adj_blocks, block_rows, block_cols, live_mask):
    hbm = pl.BlockSpec(memory_space=pl.ANY)
    vmem = pl.BlockSpec(memory_space=pltpu.VMEM)
    quad = (4, BLK, BLK)
    half = (4, HALF, BLK)
    scratch = [
        pltpu.VMEM((SLOTS, BLK, BLK), BF),
        pltpu.VMEM((SLOTS, BLK, BLK), BF),
        pltpu.VMEM(quad, BF),
        pltpu.VMEM((BLOCKS, HALF, BLK), BF),
        pltpu.VMEM((BLOCKS, HALF, BLK), BF),
        pltpu.VMEM((2, SLOTS + 1, HALF, BLK), F32),
        pltpu.VMEM((2, BLOCKS, HALF, BLK), BF),
        pltpu.VMEM((BLOCKS, HALF, BLK), BF),
        pltpu.VMEM((BLOCKS, HALF, BLK), BF),
        pltpu.VMEM((2, BLOCKS, HALF, BLK), BF),
        pltpu.VMEM((BLK, 2 * BLK), BF),
        pltpu.VMEM((4, BLK, 2 * BLK), BF),
        pltpu.VMEM((4, BLK, 2 * BLK), BF),
        pltpu.VMEM((4, BLK, 2 * BLK), BF),
        pltpu.VMEM(quad, BF),
        pltpu.VMEM(quad, BF),
        pltpu.VMEM(quad, BF),
        pltpu.VMEM((2, 4, 2, HALF, BLK), BF),
        pltpu.VMEM((2, 4, 2, HALF, BLK), BF),
        pltpu.VMEM((2, 4) + half, BF),
        pltpu.VMEM((2, 4) + half, BF),
        pltpu.VMEM((2, 3) + half, BF),
        pltpu.VMEM((2, 3) + half, BF),
        pltpu.VMEM((2,) + half, F32),
        pltpu.VMEM((2, 8) + half, BF),
        pltpu.VMEM((2, 2, 2, HALF, BLK), BF),
        pltpu.VMEM((2, 2, 2, HALF, BLK), BF),
        pltpu.VMEM((2, 2) + half, BF),
        pltpu.VMEM((2, 2) + half, BF),
        pltpu.VMEM((2,) + half, BF),
        pltpu.VMEM((2,) + half, BF),
        pltpu.VMEM((BLK, 2 * BLK), F32),
        pltpu.VMEM((3, 32, 2 * BLK), F32),
        pltpu.VMEM((32, 2 * BLK), F32),
        pltpu.VMEM((3, 8, 2 * BLK), F32),
        pltpu.VMEM((4, 8, 2 * BLK), F32),
        pltpu.VMEM((8, 2 * BLK), F32),
        pltpu.VMEM((8, 2 * BLK), F32),
        pltpu.VMEM((8, 2 * BLK), F32),
        pltpu.VMEM((8, 2 * BLK), F32),
        pltpu.VMEM((BLK, 2 * BLK), F32),
        pltpu.VMEM((8, SLOTS), jnp.int32),
        pltpu.SMEM((8, SLOTS), jnp.int32),
        pltpu.SemaphoreType.DMA((192,)),
        pltpu.SemaphoreType.DMA((192,)),
        pltpu.SemaphoreType.DMA((8,)),
    ]
    outs = (
        jax.ShapeDtypeStruct((4, BLK, 2 * BLK), BF),
        jax.ShapeDtypeStruct(quad, BF),
        jax.ShapeDtypeStruct((BLK, 2 * BLK), F32),
    )
    held = pl.pallas_call(
        kernel,
        out_shape=outs,
        in_specs=[hbm, hbm, hbm, hbm, vmem, vmem, vmem],
        out_specs=(hbm, hbm, hbm),
        scratch_shapes=scratch,
        compiler_params=pltpu.CompilerParams(
            collective_id=0, has_side_effects=True, vmem_limit_bytes=60 << 20
        ),
        cost_estimate=pl.CostEstimate(flops=2 << 30, bytes_accessed=12 << 20, transcendentals=1 << 17),
        name="graph_layer",
    )(
        features.reshape(quad),
        weight,
        cotangent.reshape(4, BLK, 2 * BLK),
        adj_blocks.reshape(SLOTS, BLK, BLK),
        block_rows.reshape(1, SLOTS),
        block_cols.reshape(1, SLOTS),
        live_mask.reshape(1, SLOTS),
    )
    act, gi, gw = pl.pallas_call(
        leave,
        out_shape=outs,
        in_specs=[hbm] * 3,
        out_specs=(vmem,) * 3,
        scratch_shapes=[pltpu.SemaphoreType.DMA((3,))],
        name="leave",
    )(*held)
    return act.reshape(4 * BLK, 2 * BLK), gi.reshape(4 * BLK, BLK), gw


def solution(mesh):
    in_specs = (
        P(("col", "row"), None),
        P(),
        P(("row", "col"), None),
        P("row", "col", None, None, None),
        P("row", "col", None),
        P("row", "col", None),
        P("row", "col", None),
    )
    out_specs = (P(("row", "col"), None), P(("col", "row"), None), P())
    return jax.shard_map(
        on_device, mesh=mesh, in_specs=in_specs, out_specs=out_specs, check_vma=False
    )
```

time: 110 us -> 98 us (0.89)
  Pallas kernels: 104 us -> 96.7 us
  local copies, waits for them, and re-layouts: 4.8 us -> 0 us
    pallas_call x1 -> x2, Pallas kernels: 104 us -> 96.7 us  [the longest x1 94.8 us: on_device(): pl.pallas_call(kernel, out_shape=outs, in_specs=[hbm, hbm, hbm, hbm, vmem...]
    unnamed x3 -> x0, local copies, waits for them, and re-layouts: 4.8 us -> none
where the time goes in v2:
time: 98 us; the launch traced here: 97.3 us
  Pallas kernels  96.7 us (99%)
    pallas_call x1, Pallas kernels, on_device(): pl.pallas_call(kernel, out_shape=outs, in_specs=[hbm, hbm, hbm, hbm, vmem...  94.8 us

profile of v2, /device:TPU:1, one launch (start us, length us, event | category | flops | bytes accessed | tf_op | source)
XLA Modules:
  0.0 97.3 jit_solution(11739795155233910069)
XLA Ops:
  0.6 94.8 %graph_layer.1 = (bf16[4,128,256]{2,1,0:T(8,128)(2,1)}, bf16[4,128,128]{2,1,0:T(8,128)(2,1)}, f32[128,256]{1,0:T(8,128)}) custom-call(bf16[4,128,128]{2,1,0:T(8,128)(2,1)} %bitcast.10, bf16[128,256]{1,0:T(8,128)(2,1)} %weight.1, bf16[4,128,256]{2,1,0:T(8,128)(2,1)} %bitcast.9, bf16[256,128,128]{2,1,0:T(8,128)(2,1)} %bitcast.8, s32[1,256]{1,0:T(1,128)} %bitcast.11, ...), custom_call_target="tpu_custom_call" | custom-call | flops 2147483648 | bytes 12582912 | tf_op jit(solution)/shard_map/graph_layer/pallas_call | solution.py:711
  95.5 1.9 %leave.1 = (bf16[4,128,256]{2,1,0:T(8,128)(2,1)}, bf16[4,128,128]{2,1,0:T(8,128)(2,1)}, f32[128,256]{1,0:T(8,128)}) custom-call(bf16[4,128,256]{2,1,0:T(8,128)(2,1)} %get-tuple-element.9.act, bf16[4,128,128]{2,1,0:T(8,128)(2,1)} %get-tuple-element.10.gi, f32[128,256]{1,0:T(8,128)} %get-tuple-element.11.gw), custom_call_target="tpu_custom_call" | custom-call | tf_op jit(solution)/shard_map/leave/pallas_call | solution.py:731

commit v3 on v2

--- a/solution.py
+++ b/solution.py
@@ -47,7 +47,7 @@
     act_out, gi_out, gw_out,
     a_v, at_v, f_v, x_0, x_1, s_v, p_v, g_0, g_1, p2_v, w_v, cot_v, act_v, gp_v, hi_v, lo_v, gi_v,
     rl, rr, rxl, rxr, zs, rz, tz,
-    sib, rl2, rr2, rxl2, rxr2, zs2, rz2,
+    sib, ro2, rl2, rr2, rxl2, rxr2, zs2, rz2,
     gwp, gx, g1, gz, gy, g3, gc, g4, gh, gwf,
     tab_v, tab, send_sem, recv_sem, local_sem,
 ):
@@ -508,30 +508,40 @@
     def both(f, i, b):
         return partial2(f, chunk_of(i), b) + sib[f, i, b].astype(F32)
 
-    def emit(name, f, i, lo, value, to, device):
+    def emit(name, f, i, lo, value, to, device, n=2):
         chunk = chunk_of(i)
 
         def body(b):
             p2_v[f, chunk * 4 + lo + b] = value(b).astype(BF)
 
-        each(0, 2, body)
-        send(name, part(p2_v, f, chunk, lo, lo + 2), to, device)
+        each(0, n, body)
+        send(name, part(p2_v, f, chunk, lo, lo + n), to, device)
 
     def relay2(f, g):
         i = 4 * g
         halved(f, i)
+        if g == 0:
+            emit(f"Ewo{f}", f, i, 0, lambda b: both(f, i, b), ro2.at[f], over, 4)
+            return
         emit(f"Err{f}{g}", f, i, 0, lambda b: both(f, i, b), rl2.at[f, g], up)
         emit(f"Erl{f}{g}", f, i, 2, lambda b: both(f, i, b + 2), rr2.at[f, g], down)
 
     def raw2(f, g):
         i = 4 * g + 1
         halved(f, i)
+        if g == 0:
+            emit(f"Ewr{f}0", f, i, 0, lambda b: both(f, i, b), rxl2.at[f, 0], up, 4)
+            halved(f, i + 1)
+            emit(f"Ewl{f}0", f, i + 1, 0, lambda b: both(f, i + 1, b), rxr2.at[f, 0], down, 4)
+            return
         emit(f"Ewr{f}{g}", f, i, 2, lambda b: both(f, i, b + 2), pair(rxl2, f, g, 2), up)
         k = 4 * g + 2
         halved(f, k)
         emit(f"Ewl{f}{g}", f, k, 0, lambda b: both(f, k, b), pair(rxr2, f, g, 0), down)
 
     def summed2(f, g):
+        if g == 0:
+            return
         i = 4 * g + 1
         recv(f"Err{f}{g}", rl2.at[f, g], down)
         emit(
@@ -547,6 +557,11 @@
 
     def gathered2(f, g):
         halved(f, 4 * g + 3)
+        if g == 0:
+            recv(f"Ewr{f}0", rxl2.at[f, 0], down)
+            recv(f"Ewl{f}0", rxr2.at[f, 0], up)
+            recv(f"Ewo{f}", ro2.at[f], over)
+            return
         recv(f"Ewr{f}{g}", pair(rxl2, f, g, 2), down)
         recv(f"Ewl{f}{g}", pair(rxr2, f, g, 0), up)
         recv(f"Esr{f}{g}", pair(rxl2, f, g, 0), down)
@@ -559,7 +574,7 @@
         gathered2(f, 0)
 
         def body(b):
-            zs2[f, b] = total2(f, 0, b).astype(BF)
+            zs2[f, b] = (total2(f, 0, b) + ro2[f, b].astype(F32)).astype(BF)
 
         each(0, 4, body)
         send(f"Ez{f}", zs2.at[f], rz2.at[f], across_dev)
@@ -681,6 +696,7 @@
         pltpu.VMEM((2, 3) + half, BF),
         pltpu.VMEM((2,) + half, F32),
         pltpu.VMEM((2, 8) + half, BF),
+        pltpu.VMEM((2,) + half, BF),
         pltpu.VMEM((2, 2, 2, HALF, BLK), BF),
         pltpu.VMEM((2, 2, 2, HALF, BLK), BF),
         pltpu.VMEM((2, 2) + half, BF),

time: 98 us -> 97.1 us (level)
  no operation moved by 1% of the time
where the time goes in v3:
time: 97.1 us; the launch traced here: 96.8 us
  Pallas kernels  96.2 us (99%)
    pallas_call x1, Pallas kernels, on_device(): pl.pallas_call(kernel, out_shape=outs, in_specs=[hbm, hbm, hbm, hbm, vmem...  94.3 us

profile of v3, /device:TPU:1, one launch (start us, length us, event | category | flops | bytes accessed | tf_op | source)
XLA Modules:
  0.0 96.8 jit_solution(6327851408013284704)
XLA Ops:
  0.6 94.3 %graph_layer.1 = (bf16[4,128,256]{2,1,0:T(8,128)(2,1)}, bf16[4,128,128]{2,1,0:T(8,128)(2,1)}, f32[128,256]{1,0:T(8,128)}) custom-call(bf16[4,128,128]{2,1,0:T(8,128)(2,1)} %bitcast.10, bf16[128,256]{1,0:T(8,128)(2,1)} %weight.1, bf16[4,128,256]{2,1,0:T(8,128)(2,1)} %bitcast.9, bf16[256,128,128]{2,1,0:T(8,128)(2,1)} %bitcast.8, s32[1,256]{1,0:T(1,128)} %bitcast.11, ...), custom_call_target="tpu_custom_call" | custom-call | flops 2147483648 | bytes 12582912 | tf_op jit(solution)/shard_map/graph_layer/pallas_call | solution.py:727
  95.0 1.9 %leave.1 = (bf16[4,128,256]{2,1,0:T(8,128)(2,1)}, bf16[4,128,128]{2,1,0:T(8,128)(2,1)}, f32[128,256]{1,0:T(8,128)}) custom-call(bf16[4,128,256]{2,1,0:T(8,128)(2,1)} %get-tuple-element.9.act, bf16[4,128,128]{2,1,0:T(8,128)(2,1)} %get-tuple-element.10.gi, f32[128,256]{1,0:T(8,128)} %get-tuple-element.11.gw), custom_call_target="tpu_custom_call" | custom-call | tf_op jit(solution)/shard_map/leave/pallas_call | solution.py:747
